TPU v7x, 32 devices: a whole 2x2x4 slice. The times are simulated.
32 devices in a mesh: group: 4 (over y, x), ctx: 8 (over z, core).
Axes of the slice: x: 2, y: 2, z: 4, core: 2. Of those that a mesh axis runs over, the one named last changes fastest.
Arguments:
- query: bfloat16 [128, 128, 576], P('group', 'ctx'), may hold values from -160 to 160
- cache: bfloat16 [32, 8192, 576], P('group', 'ctx'), may hold values from -6 to 6
- new_keys: bfloat16 [128, 576], P('group'), may hold values from -7 to 7
- lengths: int32 [32], P('group'), may hold values from 1 to 8192, as said below
- value_up_weight: bfloat16 [128, 512, 128], P('ctx'), may hold values from -1 to 1
- w_out: bfloat16 [16384, 7168], P('ctx'), may hold values from -0.1875 to 0.1875
- residual: bfloat16 [128, 7168], P(('group', 'ctx')), may hold values from -6 to 6
- norm_gain: float32 [7168], replicated, may hold values from 0.1 to 1.9
- w_router: bfloat16 [7168, 16], replicated, may hold values from -0.125 to 0.125
- routes: int32 [128, 8], P(('group', 'ctx')), may hold values from 0 to 15, all different within a row
- w_gate: bfloat16 [7168, 32768], P(None, ('group', 'ctx')), may hold values from -0.0625 to 0.0625
- w_up: bfloat16 [7168, 32768], P(None, ('group', 'ctx')), may hold values from -0.0625 to 0.0625
- w_down: bfloat16 [32768, 7168], P(('group', 'ctx')), may hold values from -0.125 to 0.125
Outputs:
- attn_out: bfloat16 [128, 7168], P(('group', 'ctx'))
- layer_out: bfloat16 [128, 7168], P(('group', 'ctx'))
Inputs may be any that keep to these rules, and one draw needn't show every extreme that they name: `lengths`: some request has all 8192 positions live.
All inputs are finite; a program needn't handle non-finite values.
Results may differ from a plain program's by a relative error of at most 0.018.
Values may be sent and summed in bfloat16 or wider, within the bound.
A program may use at most 192 MiB of HBM per device.

v0:
```python
import jax
import jax.numpy as jnp
from jax import lax
from jax.sharding import PartitionSpec as P

LATENT_WIDTH = 512
ROTARY_WIDTH = 64
QK_NOPE = 128
VALUE_HEAD_WIDTH = 128
EXPERTS = 16


neg_floor = -1e30
route_scale = 2.5
norm_eps = 1e-06


def expert_partial(slot_rows, w_gate, w_up, w_down):
    gate_sum = jnp.dot(slot_rows, w_gate, preferred_element_type=jnp.float32)
    up_sum = jnp.dot(slot_rows, w_up, preferred_element_type=jnp.float32)
    hidden = (jax.nn.silu(gate_sum) * up_sum).astype(jnp.bfloat16)
    return jnp.dot(hidden, w_down, preferred_element_type=jnp.float32)


def local(
    query,
    cache,
    new_keys,
    lengths,
    value_up_weight,
    w_out,
    residual,
    norm_gain,
    w_router,
    routes,
    w_gate,
    w_up,
    w_down,
):
    score_scale = (QK_NOPE + ROTARY_WIDTH) ** (-0.5)
    ctx_count = lax.axis_size("ctx")
    group_count = lax.axis_size("group")
    ctx_index = lax.axis_index("ctx")
    grouped_rows, local_heads, features = query.shape
    request_batch = lengths.shape[0]
    draft_tokens = grouped_rows // request_batch
    block_len = cache.shape[1]
    positions = ctx_index * block_len + jnp.arange(block_len, dtype=jnp.int32)
    live_mask = (positions[None, :] < lengths[:, None])[:, None, None, :]
    compressed_keys = cache[:, :, :LATENT_WIDTH]
    all_heads = lax.all_gather(query, "ctx", axis=1, tiled=True)
    current_width = all_heads.shape[1]
    shaped = all_heads.reshape(request_batch, draft_tokens, current_width, features)
    scores = score_scale * jnp.einsum(
        "rqhd,rtd->rqht", shaped, cache, preferred_element_type=jnp.float32
    )
    block_max = jnp.max(jnp.where(live_mask, scores, neg_floor), axis=-1)
    probability = jnp.exp(jnp.where(live_mask, scores - block_max[..., None], neg_floor))
    block_sum = jnp.sum(probability, axis=-1)
    block_result = jnp.einsum(
        "rqht,rtk->rqhk",
        probability.astype(jnp.bfloat16),
        compressed_keys,
        preferred_element_type=jnp.float32,
    )
    arrived = (
        lax.all_to_all(
            block_max.reshape(grouped_rows, current_width)[None],
            "ctx",
            split_axis=2,
            concat_axis=0,
            tiled=True,
        ),
        lax.all_to_all(
            block_sum.reshape(grouped_rows, current_width)[None],
            "ctx",
            split_axis=2,
            concat_axis=0,
            tiled=True,
        ),
        lax.all_to_all(
            block_result.reshape(grouped_rows, current_width, LATENT_WIDTH)[None],
            "ctx",
            split_axis=2,
            concat_axis=0,
            tiled=True,
        ),
    )
    cache_max = jnp.max(arrived[0], axis=0)
    factors = jnp.exp(arrived[0] - cache_max[None])
    cache_sum = jnp.sum(factors * arrived[1], axis=0)
    cache_result = jnp.sum(factors[..., None] * arrived[2], axis=0)
    own_query = query.reshape(request_batch, draft_tokens, local_heads, features)
    recent_keys = new_keys.reshape(request_batch, draft_tokens, features)
    near_scores = score_scale * jnp.einsum(
        "rqhd,rjd->rqhj", own_query, recent_keys, preferred_element_type=jnp.float32
    )
    causal = (
        jnp.arange(draft_tokens, dtype=jnp.int32)[None, :]
        <= jnp.arange(draft_tokens, dtype=jnp.int32)[:, None]
    )
    causal = causal[None, :, None, :]
    near_max = jnp.max(jnp.where(causal, near_scores, neg_floor), axis=-1)
    shaped_max = cache_max.reshape(request_batch, draft_tokens, local_heads)
    joint_max = jnp.maximum(shaped_max, near_max)
    cache_rescale = jnp.exp(shaped_max - joint_max)
    nearby_probability = jnp.exp(jnp.where(causal, near_scores - joint_max[..., None], neg_floor))
    denominator = cache_sum.reshape(
        request_batch, draft_tokens, local_heads
    ) * cache_rescale + jnp.sum(nearby_probability, axis=-1)
    softmax_numerator = cache_result.reshape(
        request_batch, draft_tokens, local_heads, LATENT_WIDTH
    ) * cache_rescale[..., None] + jnp.einsum(
        "rqhj,rjk->rqhk",
        nearby_probability,
        recent_keys[:, :, :LATENT_WIDTH].astype(jnp.float32),
        precision=lax.Precision.HIGHEST,
    )
    latent_vector = (
        (softmax_numerator / denominator[..., None])
        .astype(jnp.bfloat16)
        .reshape(grouped_rows, local_heads, LATENT_WIDTH)
    )
    per_head_values = jnp.einsum(
        "gxj,xjs->gxs", latent_vector, value_up_weight, preferred_element_type=jnp.float32
    )
    per_head_values = per_head_values.astype(jnp.bfloat16).reshape(
        grouped_rows, local_heads * VALUE_HEAD_WIDTH
    )
    row_count = residual.shape[0]
    attention = lax.psum_scatter(
        jnp.dot(per_head_values, w_out, preferred_element_type=jnp.float32).astype(jnp.bfloat16),
        "ctx",
        scatter_dimension=0,
        tiled=True,
    ).astype(jnp.float32)
    attn_out = attention.astype(jnp.bfloat16)
    stream = (residual.astype(jnp.float32) + attention).astype(jnp.bfloat16)
    stream_wide = stream.astype(jnp.float32)
    mean_square = jnp.mean(stream_wide * stream_wide, axis=-1, keepdims=True)
    normed = (stream_wide * lax.rsqrt(mean_square + norm_eps) * norm_gain).astype(jnp.bfloat16)
    gate_values = jax.nn.sigmoid(jnp.dot(normed, w_router, preferred_element_type=jnp.float32))
    expert_ids = jnp.arange(EXPERTS, dtype=jnp.int32)
    selected_experts = (routes[:, :, None] == expert_ids[None, None, :]).astype(jnp.float32)
    picked = jnp.sum(selected_experts * gate_values[:, None, :], axis=-1)
    route_weights = route_scale * picked / jnp.sum(picked, axis=-1, keepdims=True)
    device_count = group_count * ctx_count
    slices = device_count // EXPERTS
    owners = jnp.arange(device_count, dtype=jnp.int32) // slices
    row_ids = jnp.arange(row_count, dtype=jnp.int32)
    earlier = row_ids[:, None] > row_ids[None, :]
    same_expert = routes[:, :, None, None] == routes[None, None, :, :]
    slot_index = jnp.sum((same_expert & earlier[:, None, :, None]).astype(jnp.int32), axis=(2, 3))
    targets = (routes[:, :, None] == owners[None, None, :])[..., None] & (
        slot_index[:, :, None, None] == row_ids[None, None, None, :]
    )
    placing = jnp.sum(targets.astype(jnp.float32), axis=1)
    coefficient = jnp.sum(route_weights[:, :, None, None] * targets.astype(jnp.float32), axis=1)
    outgoing = jnp.einsum(
        "idc,ij->dcj", placing.astype(jnp.bfloat16), normed, preferred_element_type=jnp.float32
    ).astype(jnp.bfloat16)
    model_width = residual.shape[1]
    slot_block = lax.all_to_all(outgoing, ("group", "ctx"), split_axis=0, concat_axis=0, tiled=True)
    slot_span = slot_block.shape[1]
    partial_out = expert_partial(
        slot_block.reshape(device_count * slot_span, model_width), w_gate, w_up, w_down
    )
    returned = lax.all_to_all(
        partial_out.reshape(device_count, slot_span, model_width).astype(jnp.bfloat16),
        ("group", "ctx"),
        split_axis=0,
        concat_axis=0,
        tiled=True,
    ).astype(jnp.float32)
    expert_mix = jnp.einsum("idc,dcj->ij", coefficient, returned, precision=lax.Precision.HIGHEST)
    layer_out = (stream_wide + expert_mix).astype(jnp.bfloat16)
    return (attn_out, layer_out)


def solution(mesh):
    return jax.shard_map(
        local,
        mesh=mesh,
        in_specs=(
            P("group", "ctx", None),
            P("group", "ctx", None),
            P("group", None),
            P("group"),
            P("ctx", None, None),
            P("ctx", None),
            P(("group", "ctx"), None),
            P(),
            P(),
            P(("group", "ctx"), None),
            P(None, ("group", "ctx")),
            P(None, ("group", "ctx")),
            P(("group", "ctx"), None),
        ),
        out_specs=(P(("group", "ctx"), None), P(("group", "ctx"), None)),
        check_vma=False,
    )
```

profile of v0, /device:TPU:0, one launch (start us, length us, event | category | flops | bytes accessed | tf_op | source)
XLA Modules:
  0.0 529.6 jit_solution(12806113474802893608)
XLA Ops:
  8.7 59.7 %all-gather.2.cloned.1.call-done = bf16[32,128,576]{2,1,0:T(8,128)(2,1)} async-done(((bf16[32,16,576]{2,1,0:T(8,128)(2,1)}), bf16[32,128,576]{2,1,0:T(8,128)(2,1)}) %all-gather.2.cloned.1.call-update) | async-done | bytes 4718608 | tf_op jit(solution)/shard_map/all_gather | solution.py:51
  68.4 10.7 %select_reduce_fusion = (f32[8,4,128]{2,1,0:T(4,128)S(1)}, f32[8,4,128,1024]{3,2,1,0:T(8,128)S(1)}) fusion(pred[8,1024]{1,0:T(8,128)(4,1)S(1)} %broadcast_compare_fusion, bf16[8,4,128,576]{3,2,1,0:T(8,128)(2,1)} %bitcast.102, bf16[8,1024,576]{1,2,0:T(8,128)(2,1)} %param.14), kind=kOutput, calls=%fused_computation.1 | convolution fusion | flops 4844417024 | bytes 30957568 | tf_op jit(solution)/shard_map/rqhd,rtd->rqht/dot_general | solution.py:54
  79.1 5.7 %copy-done.3 = f32[8,4,128,1024]{3,2,1,0:T(8,128)} copy-done((f32[8,4,128,1024]{3,2,1,0:T(8,128)}, f32[8,4,128,1024]{3,2,1,0:T(8,128)S(1)}, u32[]{:S(2)}) %copy-start.3) | copy-done | bytes 16777240
  84.8 4.4 fusion
  91.3 3.3 all-to-all-start.2
  96.2 4.0 all-to-all-done.2
  100.2 3.5 all-to-all-start
  103.8 13.0 %fusion.4 = f32[8,4,128,512]{3,2,1,0:T(8,128)} fusion(f32[8,4,128,1024]{3,2,1,0:T(8,128)} %copy-done.3, bf16[8,1024,576]{1,2,0:T(8,128)(2,1)} %param.14, f32[8,4,128]{2,1,0:T(4,128)S(1)} %get-tuple-element.12, pred[8,1024]{1,0:T(8,128)(4,1)S(1)} %broadcast_compare_fusion), kind=kOutput, calls=%fused_computation.8 | convolution fusion | flops 4311744512 | bytes 33579008 | tf_op jit(solution)/shard_map/rqht,rtk->rqhk/dot_general | solution.py:60
  116.7 11.5 %copy.75 = f32[1,32,128,512]{3,1,0,2:T(8,128)} copy(f32[1,32,128,512]{3,2,1,0:T(8,128)} %bitcast.84) | data formatting | bytes 16777216 | tf_op jit(solution)/shard_map/broadcast_in_dim;reshape | solution.py:82
  128.2 5.2 all-to-all-start.1
  137.1 180.2 %all-to-all-done.1 = f32[1,32,128,512]{3,1,0,2:T(8,128)} async-done(((f32[1,32,128,512]{3,1,0,2:T(8,128)}), f32[1,32,128,512]{3,1,0,2:T(8,128)}, u32[]{:S(2)}, u32[]{:S(2)}) %all-to-all-start.1) | async-done | bytes 8388640 | tf_op jit(solution)/shard_map/all_to_all | solution.py:81
  317.3 3.9 multiply_reduce_fusion
  323.3 12.9 %convolution_convert_fusion.2 = bf16[32,7168]{1,0:T(8,128)(2,1)} fusion(bf16[2048,7168]{1,0:T(8,128)(2,1)} %param.18, bf16[16,4,8,128]{3,2,1,0:T(8,128)(2,1)S(1)} %fusion.18), kind=kOutput, calls=%fused_computation.16 | convolution fusion | flops 939753472 | bytes 29949952 | tf_op jit(solution)/shard_map/dot_general | solution.py:132
  337.6 53.4 %all-reduce.3.cloned.1.call-done = bf16[32,7168]{1,0:T(8,128)(2,1)} async-done(((bf16[32,7168]{1,0:T(8,128)(2,1)}), bf16[32,7168]{1,0:T(8,128)(2,1)}) %all-reduce.3.cloned.1.call-update) | async-done | bytes 458768
  391.0 1.1 fusion.31
  393.5 1.4 copy.83
  395.0 48.0 %all_to_all.64 = bf16[32,4,7168]{2,1,0:T(4,128)(2,1)} all-to-all(bf16[32,4,7168]{2,1,0:T(4,128)(2,1)S(1)} %copy.83), channel_id=1, replica_groups=mesh['group'=4,'ctx'=8] {'group','ctx'}, dimensions={0} | all-to-all | bytes 3670016 | tf_op jit(solution)/shard_map/all_to_all | solution.py:163
  442.9 2.9 reshape.186
  445.9 1.2 copy-done.2
  447.1 7.2 %fusion.50 = f32[128,1024]{1,0:T(8,128)S(1)} fusion(bf16[128,7168]{1,0:T(8,128)(2,1)S(1)} %reshape.186, bf16[7168,1024]{1,0:T(8,128)(2,1)} %param.23), kind=kOutput, calls=%fused_computation.88 | convolution fusion | flops 1879048192 | bytes 17039360 | tf_op jit(solution)/shard_map/dot_general | solution.py:19
  454.3 15.4 %convolution_convert_fusion = bf16[128,7168]{1,0:T(8,128)(2,1)} fusion(bf16[1024,7168]{1,0:T(8,128)(2,1)} %param.25, bf16[128,7168]{1,0:T(8,128)(2,1)} %copy-done.2, bf16[7168,1024]{1,0:T(8,128)(2,1)} %param.24, f32[128,1024]{1,0:T(8,128)S(1)} %fusion.50), kind=kOutput, calls=%fused_computation.6 | convolution fusion | flops 3759800320 | bytes 33554432 | tf_op jit(solution)/shard_map/dot_general | solution.py:22
  469.7 4.1 convert_element_type.75
  473.8 47.1 %all_to_all.65 = bf16[32,4,7168]{2,1,0:T(4,128)(2,1)S(1)} all-to-all(bf16[32,4,7168]{2,1,0:T(4,128)(2,1)} %convert_element_type.75), channel_id=1, replica_groups=mesh['group'=4,'ctx'=8] {'group','ctx'}, dimensions={0} | all-to-all | bytes 3670016 | tf_op jit(solution)/shard_map/all_to_all | solution.py:168
  520.9 1.8 fusion.13
  (66 shorter events, 12.8 us)
Async XLA Ops:
  7.2 315.5 %copy-start = (bf16[16,512,128]{2,1,0:T(8,128)(2,1)S(1)}, bf16[16,512,128]{2,1,0:T(8,128)(2,1)}, u32[]{:S(2)}) copy-start(bf16[16,512,128]{2,1,0:T(8,128)(2,1)} %param.17) | copy-start | bytes 6291460
  7.2 61.2 %all-gather.2.cloned.1.call-start = ((), (), s32[]{:S(2)}) async-start(), calls=%async_computation.5 | async-start | bytes 5898240 | tf_op jit(solution)/shard_map/all_gather | solution.py:51
  79.1 5.7 %copy-start.3 = (f32[8,4,128,1024]{3,2,1,0:T(8,128)}, f32[8,4,128,1024]{3,2,1,0:T(8,128)S(1)}, u32[]{:S(2)}) copy-start(f32[8,4,128,1024]{3,2,1,0:T(8,128)S(1)} %get-tuple-element.13) | copy-start | bytes 50331652
  91.3 8.9 %all-to-all-start.2 = ((f32[8,1,512]{2,1,0:T(1,128)}), f32[8,1,512]{2,1,0:T(1,128)S(1)}, u32[]{:S(2)}, u32[]{:S(2)}) async-start(f32[8,1,512]{2,1,0:T(1,128)} %reshape.197), calls=%async_computation.2 | async-start | bytes 32768 | tf_op jit(solution)/shard_map/all_to_all | solution.py:74
  100.2 28.0 %all-to-all-start = ((f32[8,1,512]{2,1,0:T(1,128)}), f32[8,1,512]{2,1,0:T(1,128)S(1)}, u32[]{:S(2)}, u32[]{:S(2)}) async-start(f32[8,1,512]{2,1,0:T(1,128)} %reshape.195), calls=%async_computation | async-start | bytes 32768 | tf_op jit(solution)/shard_map/all_to_all | solution.py:67
  128.2 5.5 %copy-start.7 = (bf16[32,576]{1,0:T(8,128)(2,1)S(1)}, bf16[32,576]{1,0:T(8,128)(2,1)}, u32[]{:S(2)}) copy-start(bf16[32,576]{1,0:T(8,128)(2,1)} %param.15) | copy-start | bytes 110596
  128.2 5.6 %copy-start.8 = (s32[4,8]{1,0:T(4,128)S(1)}, s32[4,8]{1,0:T(4,128)}, u32[]{:S(2)}) copy-start(s32[4,8]{1,0:T(4,128)} %param.22) | copy-start | bytes 388
  128.2 5.8 %copy-start.4 = (bf16[32,16,576]{2,1,0:T(8,128)(2,1)S(1)}, bf16[32,16,576]{2,1,0:T(8,128)(2,1)}, u32[]{:S(2)}) copy-start(bf16[32,16,576]{2,1,0:T(8,128)(2,1)} %param.13) | copy-start | bytes 1769476
  128.2 189.1 %all-to-all-start.1 = ((f32[1,32,128,512]{3,1,0,2:T(8,128)}), f32[1,32,128,512]{3,1,0,2:T(8,128)}, u32[]{:S(2)}, u32[]{:S(2)}) async-start(f32[1,32,128,512]{3,1,0,2:T(8,128)} %copy.75), calls=%async_computation.1 | async-start | bytes 16777216 | tf_op jit(solution)/shard_map/all_to_all | solution.py:81
  133.4 257.6 %all-reduce.3.cloned.1.call-start = ((), (), s32[]{:S(2)}) async-start(), calls=%async_computation.6 | async-start | bytes 917504
  323.3 13.0 %copy-start.11 = (u32[32]{0:T(128)S(1)}, u32[32]{0:T(128)}, u32[]{:S(2)}) copy-start(u32[32]{0:T(128)} %constant.49) | copy-start | bytes 388
  323.3 67.8 %copy-start.5 = (bf16[4,7168]{1,0:T(4,128)(2,1)S(1)}, bf16[4,7168]{1,0:T(4,128)(2,1)}, u32[]{:S(2)}) copy-start(bf16[4,7168]{1,0:T(4,128)(2,1)} %param.19) | copy-start | bytes 172036
  323.3 68.8 %copy-start.9 = (f32[7168]{0:T(1024)S(1)}, f32[7168]{0:T(1024)}, u32[]{:S(2)}) copy-start(f32[7168]{0:T(1024)} %param.20) | copy-start | bytes 86020
  323.3 68.8 %copy-start.10 = (bf16[7168,16]{0,1:T(8,128)(2,1)S(1)}, bf16[7168,16]{0,1:T(8,128)(2,1)}, u32[]{:S(2)}) copy-start(bf16[7168,16]{0,1:T(8,128)(2,1)} %param.21) | copy-start | bytes 688132
  392.1 128.8 %copy-start.6 = (bf16[4,7168]{1,0:T(4,128)(2,1)}, bf16[4,7168]{1,0:T(4,128)(2,1)S(1)}, u32[]{:S(2)}) copy-start(bf16[4,7168]{1,0:T(4,128)(2,1)S(1)} %get-tuple-element.7) | copy-start | bytes 172036
  445.9 1.2 copy-start.2
  454.3 68.4 %copy-start.1 = (bf16[16,512,128]{2,1,0:T(8,128)(2,1)S(1)}, bf16[16,512,128]{2,1,0:T(8,128)(2,1)}, u32[]{:S(2)}) copy-start(bf16[16,512,128]{2,1,0:T(8,128)(2,1)} %param.17) | copy-start | bytes 6291460
Sparse Core Ops, SparseCore 0:
  9.6 58.6 all-gather.1
  336.4 54.5 all-reduce.2
where the time goes:
time: 530 us
  waiting for transfers between devices  298 us (56%)
  blocking collectives  95.1 us (18%)
  matrix products  64.4 us (12%)
  local copies, waits for them, and re-layouts  30.6 us (6%)
  between operations  15.1 us (3%)
  other arithmetic  14 us (3%)
  starting transfers between devices  12.3 us (2%)
    all_to_all x1, waiting for transfers between devices, local(): lax.all_to_all(block_result.reshape(grouped_rows, current_width, LATENT_W...  180 us
    all_gather x1, waiting for transfers between devices, local(): all_heads = lax.all_gather(query, 'ctx', axis=1, tiled=True)  59.7 us
    unnamed x3, waiting for transfers between devices  54.1 us
    all_to_all x1, blocking collectives, local(): lax.all_to_all(outgoing, ('group', 'ctx'), split_axis=0, concat_axis=0, t...  48 us
    all_to_all x1, blocking collectives, local(): lax.all_to_all(partial_out.reshape(device_count, slot_span, model_width)....  47.1 us
    dot_general x1, matrix products, expert_partial(): return jnp.dot(hidden, w_down, preferred_element_type=jnp.float32)  15.4 us
    dot_general x1, matrix products, local(): jnp.einsum('rqht,rtk->rqhk', probability.astype(jnp.bfloat16), compressed...  13 us
    dot_general x1, matrix products, local(): jnp.dot(per_head_values, w_out, preferred_element_type=jnp.float32)  12.9 us
  transfers between devices with their start and end apart: 5, of which 4 were waited for; matrix products, arithmetic and copies ran while one was open for 6% of the time, Pallas kernels for 0%

commit v1 on v0

v1 whole, which is shorter than its diff:
```python
import functools

import jax
import jax.numpy as jnp
from jax import lax
from jax.experimental import pallas as pl
from jax.experimental.pallas import tpu as pltpu
from jax.sharding import PartitionSpec as P

LATENT_WIDTH = 512
ROTARY_WIDTH = 64
QK_NOPE = 128
VALUE_HEAD_WIDTH = 128
EXPERTS = 16
LANES = 128
MESH = pl.DeviceIdType.MESH


neg_floor = -1e30
route_scale = 2.5
norm_eps = 1e-06


def enter(peers):
    barrier = pltpu.get_barrier_semaphore()
    for peer in peers:
        pl.semaphore_signal(barrier, inc=1, device_id=peer, device_id_type=MESH)
    pl.semaphore_wait(barrier, len(peers))


def place(planes, depth):
    g = lax.axis_index("group")
    c = lax.axis_index("ctx")
    z, k = c // 2, c % 2
    partner = (g, z * 2 + 1 - k)
    plane = [(lax.rem(g + d, lax.axis_size("group")), c) for d in range(1, planes)]
    line = [(g, lax.rem(z + d, depth) * 2 + k) for d in range(1, depth)]
    return g, z, k, partner, plane, line


def gather_kernel(planes, depth, x_ref, out_ref, core_send, core_recv, plane_send, plane_recv, line_send, line_recv):
    g, z, k, partner, plane, line = place(planes, depth)
    enter([partner] + plane + line)
    out_ref[k, g, z] = x_ref[...]

    def line_copy(d, slot):
        return pltpu.make_async_remote_copy(
            src_ref=x_ref, dst_ref=slot, send_sem=line_send.at[d], recv_sem=line_recv.at[d],
            device_id=line[d - 1], device_id_type=MESH)

    def plane_copy(p, d, src, slot):
        return pltpu.make_async_remote_copy(
            src_ref=src, dst_ref=slot, send_sem=plane_send.at[p, d], recv_sem=plane_recv.at[p, d],
            device_id=plane[p - 1], device_id_type=MESH)

    def core_copy(p, d, src, slot):
        return pltpu.make_async_remote_copy(
            src_ref=src, dst_ref=slot, send_sem=core_send.at[p, d], recv_sem=core_recv.at[p, d],
            device_id=partner, device_id_type=MESH)

    sent = []
    for d in range(1, depth):
        copy = line_copy(d, out_ref.at[k, g, z])
        copy.start()
        sent.append(copy)
    for d in range(depth):
        zd = lax.rem(z - d + depth, depth)
        slot = out_ref.at[k, g, zd]
        src = x_ref if d == 0 else slot
        if d > 0:
            line_copy(d, slot).wait_recv()
        for p in range(1, planes):
            copy = plane_copy(p, d, src, slot)
            copy.start()
            sent.append(copy)
        copy = core_copy(0, d, src, slot)
        copy.start()
        sent.append(copy)
    for d in range(depth):
        zd = lax.rem(z - d + depth, depth)
        for p in range(1, planes):
            slot = out_ref.at[k, lax.rem(g - p + planes, planes), zd]
            plane_copy(p, d, slot, slot).wait_recv()
            copy = core_copy(p, d, slot, slot)
            copy.start()
            sent.append(copy)
    for d in range(depth):
        zd = lax.rem(z - d + depth, depth)
        for p in range(planes):
            slot = out_ref.at[1 - k, lax.rem(g - p + planes, planes), zd]
            core_copy(p, d, slot, slot).wait_recv()
    for copy in sent:
        copy.wait_send()


def all_rows(x, planes, depth, collective_id):
    sems = pltpu.SemaphoreType.DMA
    return pl.pallas_call(
        functools.partial(gather_kernel, planes, depth),
        out_shape=jax.ShapeDtypeStruct((2, planes, depth) + x.shape, x.dtype),
        in_specs=[pl.BlockSpec(memory_space=pltpu.VMEM)],
        out_specs=pl.BlockSpec(memory_space=pltpu.VMEM),
        scratch_shapes=[sems((planes, depth))] * 4 + [sems((depth,))] * 2,
        compiler_params=pltpu.CompilerParams(
            collective_id=collective_id, has_side_effects=True, vmem_limit_bytes=32 * 2**20),
    )(x)


def scatter_kernel(planes, depth, x_ref, out_ref, core_buf, plane_out, plane_buf, line_out, line_buf,
                   core_send, core_recv, plane_send, plane_recv, line_send, line_recv):
    g, z, k, partner, plane, line = place(planes, depth)
    enter([partner] + plane + line)
    at = g if planes > 1 else 0
    wide = lambda block: block.astype(jnp.float32)

    sent = []
    order = list(range(1, planes)) + [0]
    core = {}
    for p in order:
        gp = lax.rem(at + p, planes)
        copy = pltpu.make_async_remote_copy(
            src_ref=x_ref.at[1 - k, gp], dst_ref=core_buf.at[p], send_sem=core_send.at[p], recv_sem=core_recv.at[p],
            device_id=partner, device_id_type=MESH)
        copy.start()
        core[p] = copy
        sent.append(copy)
    planes_in = {}
    for p in order[:-1]:
        gp = lax.rem(at + p, planes)
        core[p].wait_recv()
        for d in range(depth):
            plane_out[p, d] = (wide(x_ref[k, gp, d]) + wide(core_buf[p, d])).astype(plane_out.dtype)
        copy = pltpu.make_async_remote_copy(
            src_ref=plane_out.at[p], dst_ref=plane_buf.at[p], send_sem=plane_send.at[p], recv_sem=plane_recv.at[p],
            device_id=plane[p - 1], device_id_type=MESH)
        copy.start()
        planes_in[p] = copy
        sent.append(copy)
    core[0].wait_recv()
    for p in order[:-1]:
        planes_in[p].wait_recv()

    def total(zd):
        block = wide(x_ref[k, at, zd]) + wide(core_buf[0, zd])
        for p in range(1, planes):
            block = block + wide(plane_buf[p, zd])
        return block

    lines_in = []
    for d in range(1, depth):
        line_out[d] = total(lax.rem(z + d, depth)).astype(line_out.dtype)
        copy = pltpu.make_async_remote_copy(
            src_ref=line_out.at[d], dst_ref=line_buf.at[d], send_sem=line_send.at[d], recv_sem=line_recv.at[d],
            device_id=line[d - 1], device_id_type=MESH)
        copy.start()
        lines_in.append(copy)
        sent.append(copy)
    result = total(z)
    for d in range(1, depth):
        lines_in[d - 1].wait_recv()
        result = result + wide(line_buf[d])
    out_ref[...] = result
    for copy in sent:
        copy.wait_send()


def summed_rows(x, collective_id):
    _, planes, depth, *block = x.shape
    block = tuple(block)
    sems = pltpu.SemaphoreType.DMA
    return pl.pallas_call(
        functools.partial(scatter_kernel, planes, depth),
        out_shape=jax.ShapeDtypeStruct(block, jnp.float32),
        in_specs=[pl.BlockSpec(memory_space=pltpu.VMEM)],
        out_specs=pl.BlockSpec(memory_space=pltpu.VMEM),
        scratch_shapes=[
            pltpu.VMEM((planes, depth) + block, x.dtype),
            pltpu.VMEM((planes, depth) + block, x.dtype),
            pltpu.VMEM((planes, depth) + block, x.dtype),
            pltpu.VMEM((depth,) + block, x.dtype),
            pltpu.VMEM((depth,) + block, x.dtype),
        ] + [sems((planes,))] * 4 + [sems((depth,))] * 2,
        compiler_params=pltpu.CompilerParams(
            collective_id=collective_id, has_side_effects=True, vmem_limit_bytes=32 * 2**20),
    )(x)


def local(
    query,
    cache,
    new_keys,
    lengths,
    value_up_weight,
    w_out,
    residual,
    norm_gain,
    w_router,
    routes,
    w_gate,
    w_up,
    w_down,
):
    score_scale = (QK_NOPE + ROTARY_WIDTH) ** (-0.5)
    ctx_count = lax.axis_size("ctx")
    group_count = lax.axis_size("group")
    depth = ctx_count // 2
    ctx_index = lax.axis_index("ctx")
    group_index = lax.axis_index("group")
    grouped_rows, local_heads, features = query.shape
    request_batch = lengths.shape[0]
    draft_tokens = grouped_rows // request_batch
    block_len = cache.shape[1]
    all_routes = lax.all_gather(routes, ("group", "ctx"), axis=0, tiled=True)
    positions = ctx_index * block_len + jnp.arange(block_len, dtype=jnp.int32)
    live_mask = (positions[None, :] < lengths[:, None])[:, None, None, :]
    compressed_keys = cache[:, :, :LATENT_WIDTH]
    all_heads = lax.all_gather(query, "ctx", axis=1, tiled=True)
    current_width = all_heads.shape[1]
    shaped = all_heads.reshape(request_batch, draft_tokens, current_width, features)
    scores = score_scale * jnp.einsum(
        "rqhd,rtd->rqht", shaped, cache, preferred_element_type=jnp.float32
    )
    block_max = jnp.max(jnp.where(live_mask, scores, neg_floor), axis=-1)
    probability = jnp.exp(jnp.where(live_mask, scores - block_max[..., None], neg_floor))
    block_sum = jnp.sum(probability, axis=-1)
    block_result = jnp.einsum(
        "rqht,rtk->rqhk",
        probability.astype(jnp.bfloat16),
        compressed_keys,
        preferred_element_type=jnp.float32,
    ).astype(jnp.bfloat16)
    swap = functools.partial(lax.all_to_all, axis_name="ctx", split_axis=2, concat_axis=0, tiled=True)
    arrived = (
        swap(block_max.reshape(grouped_rows, current_width)[None]),
        swap(block_sum.reshape(grouped_rows, current_width)[None]),
        swap(block_result.reshape(grouped_rows, current_width, LATENT_WIDTH)[None]),
    )
    cache_max = jnp.max(arrived[0], axis=0)
    factors = jnp.exp(arrived[0] - cache_max[None])
    cache_sum = jnp.sum(factors * arrived[1], axis=0)
    cache_result = jnp.sum(factors[..., None] * arrived[2].astype(jnp.float32), axis=0)
    own_query = query.reshape(request_batch, draft_tokens, local_heads, features)
    recent_keys = new_keys.reshape(request_batch, draft_tokens, features)
    near_scores = score_scale * jnp.einsum(
        "rqhd,rjd->rqhj", own_query, recent_keys, preferred_element_type=jnp.float32
    )
    causal = (
        jnp.arange(draft_tokens, dtype=jnp.int32)[None, :]
        <= jnp.arange(draft_tokens, dtype=jnp.int32)[:, None]
    )
    causal = causal[None, :, None, :]
    near_max = jnp.max(jnp.where(causal, near_scores, neg_floor), axis=-1)
    shaped_max = cache_max.reshape(request_batch, draft_tokens, local_heads)
    joint_max = jnp.maximum(shaped_max, near_max)
    cache_rescale = jnp.exp(shaped_max - joint_max)
    nearby_probability = jnp.exp(jnp.where(causal, near_scores - joint_max[..., None], neg_floor))
    denominator = cache_sum.reshape(
        request_batch, draft_tokens, local_heads
    ) * cache_rescale + jnp.sum(nearby_probability, axis=-1)
    softmax_numerator = cache_result.reshape(
        request_batch, draft_tokens, local_heads, LATENT_WIDTH
    ) * cache_rescale[..., None] + jnp.einsum(
        "rqhj,rjk->rqhk",
        nearby_probability,
        recent_keys[:, :, :LATENT_WIDTH].astype(jnp.float32),
        precision=lax.Precision.HIGHEST,
    )
    latent_vector = (
        (softmax_numerator / denominator[..., None])
        .astype(jnp.bfloat16)
        .reshape(grouped_rows, local_heads, LATENT_WIDTH)
    )
    per_head_values = jnp.einsum(
        "gxj,xjs->gxs", latent_vector, value_up_weight, preferred_element_type=jnp.float32
    )
    per_head_values = per_head_values.astype(jnp.bfloat16).reshape(
        grouped_rows, local_heads * VALUE_HEAD_WIDTH
    )
    row_count, model_width = residual.shape
    block = row_count * model_width // LANES
    share = jnp.dot(per_head_values, w_out, preferred_element_type=jnp.float32).astype(jnp.bfloat16)
    share = share.reshape(1, depth, 2, block, LANES).transpose(2, 0, 1, 3, 4)
    attention = summed_rows(share, 0).reshape(row_count, model_width)
    attn_out = attention.astype(jnp.bfloat16)
    stream = (residual.astype(jnp.float32) + attention).astype(jnp.bfloat16)
    stream_wide = stream.astype(jnp.float32)
    mean_square = jnp.mean(stream_wide * stream_wide, axis=-1, keepdims=True)
    normed = (stream_wide * lax.rsqrt(mean_square + norm_eps) * norm_gain).astype(jnp.bfloat16)
    rows = all_rows(normed.reshape(block, LANES), group_count, depth, 1)
    device_count = group_count * ctx_count
    rows = rows.transpose(1, 2, 0, 3, 4).reshape(device_count * row_count, model_width)
    gate_values = jax.nn.sigmoid(jnp.dot(rows, w_router, preferred_element_type=jnp.float32))
    expert_ids = jnp.arange(EXPERTS, dtype=jnp.int32)
    chosen = jnp.sum((all_routes[:, :, None] == expert_ids).astype(jnp.float32), axis=1)
    picked = chosen * gate_values
    expert = (group_index * ctx_count + ctx_index) // (device_count // EXPERTS)
    own = (expert_ids == expert).astype(jnp.float32)
    coefficient = (
        route_scale * jnp.sum(picked * own, axis=-1, keepdims=True) / jnp.sum(picked, axis=-1, keepdims=True)
    )
    gate_sum = jnp.dot(rows, w_gate, preferred_element_type=jnp.float32)
    up_sum = jnp.dot(rows, w_up, preferred_element_type=jnp.float32)
    hidden = (jax.nn.silu(gate_sum) * up_sum).astype(jnp.bfloat16)
    mixed = coefficient * jnp.dot(hidden, w_down, preferred_element_type=jnp.float32)
    mixed = mixed.astype(jnp.bfloat16).reshape(group_count, depth, 2, block, LANES)
    expert_mix = summed_rows(mixed.transpose(2, 0, 1, 3, 4), 2).reshape(row_count, model_width)
    layer_out = (stream_wide + expert_mix).astype(jnp.bfloat16)
    return (attn_out, layer_out)


def solution(mesh):
    return jax.shard_map(
        local,
        mesh=mesh,
        in_specs=(
            P("group", "ctx", None),
            P("group", "ctx", None),
            P("group", None),
            P("group"),
            P("ctx", None, None),
            P("ctx", None),
            P(("group", "ctx"), None),
            P(),
            P(),
            P(("group", "ctx"), None),
            P(None, ("group", "ctx")),
            P(None, ("group", "ctx")),
            P(("group", "ctx"), None),
        ),
        out_specs=(P(("group", "ctx"), None), P(("group", "ctx"), None)),
        check_vma=False,
    )
```

time: 530 us -> 363 us (0.68)
  waiting for transfers between devices: 298 us -> 64.4 us
  Pallas kernels: 0 us -> 48.4 us
  blocking collectives: 95.1 us -> 123 us
    all_to_all x3, waiting for transfers between devices: 184 us -> 4.01 us  [the longest x1 4.01 us: local(): swap(block_sum.reshape(grouped_rows, current_width)[None])]
    all_gather x0 -> x1, blocking collectives: none -> 123 us  [local(): all_routes = lax.all_gather(routes, ('group', 'ctx'), axis=0, tiled=True)]
    all_to_all x2 -> x0, blocking collectives: 95.1 us -> none  [the longest x1 48 us: local(): lax.all_to_all(outgoing, ('group', 'ctx'), split_axis=0, concat_axis=0, t...]
    unnamed x3 -> x1, waiting for transfers between devices: 54.1 us -> 0.68 us
    pallas_call x0 -> x3, Pallas kernels: none -> 48.4 us  [the longest x2 32.2 us: summed_rows(): pl.pallas_call(functools.partial(scatter_kernel, planes, depth), out_shap...]
    reshape x1 -> x8, local copies, waits for them, and re-layouts: 2.94 us -> 8.87 us  [the longest x2 5.58 us: local(): mixed.astype(jnp.bfloat16).reshape(group_count, depth, 2, block, LANES)]
    convert_element_type x2 -> x0, local copies, waits for them, and re-layouts: 5.47 us -> none  [the longest x1 4.06 us: local(): partial_out.reshape(device_count, slot_span, model_width)]
    dot_general x5 -> x3, matrix products: 25.4 us -> 23.9 us  [the longest x1 15.4 us: local(): jnp.dot(hidden, w_down, preferred_element_type=jnp.float32)]
  transfers between devices with their start and end apart: 5 -> 4, of which waited for: 4 -> 2; matrix products, arithmetic and copies ran while one was open for 6% -> 7% of each run, Pallas kernels for 0% -> 0%
where the time goes in v1:
time: 363 us; the launch traced here: 362 us
  blocking collectives  123 us (34%)
  waiting for transfers between devices  64.4 us (18%)
  matrix products  61.6 us (17%)
  Pallas kernels  48.4 us (13%)
  local copies, waits for them, and re-layouts  25.9 us (7%)
  between operations  14.5 us (4%)
  other arithmetic  12.6 us (3%)
  starting transfers between devices  11.8 us (3%)
    all_gather x1, blocking collectives, local(): all_routes = lax.all_gather(routes, ('group', 'ctx'), axis=0, tiled=True)  123 us
    all_gather x1, waiting for transfers between devices, local(): all_heads = lax.all_gather(query, 'ctx', axis=1, tiled=True)  59.7 us
    pallas_call x2, Pallas kernels, summed_rows(): pl.pallas_call(functools.partial(scatter_kernel, planes, depth), out_shap...  32.2 us
    pallas_call x1, Pallas kernels, all_rows(): pl.pallas_call(functools.partial(gather_kernel, planes, depth), out_shape...  16.3 us
    dot_general x1, matrix products, local(): jnp.dot(hidden, w_down, preferred_element_type=jnp.float32)  15.4 us
    dot_general x1, matrix products, local(): jnp.einsum('rqht,rtk->rqhk', probability.astype(jnp.bfloat16), compressed...  12.4 us
    dot_general x1, matrix products, local(): jnp.dot(per_head_values, w_out, preferred_element_type=jnp.float32)  12.1 us
    dot_general x1, matrix products, local(): jnp.einsum('rqhd,rtd->rqht', shaped, cache, preferred_element_type=jnp.fl...  10.7 us
  transfers between devices with their start and end apart: 4, of which 2 were waited for; matrix products, arithmetic and copies ran while one was open for 7% of the time, Pallas kernels for 0%

profile of v1, /device:TPU:0, one launch (start us, length us, event | category | flops | bytes accessed | tf_op | source)
XLA Modules:
  0.0 362.4 jit_solution(14394674227497178152)
XLA Ops:
  8.7 59.7 %all-gather.3.cloned.1.call-done = bf16[32,128,576]{2,1,0:T(8,128)(2,1)} async-done(((bf16[32,16,576]{2,1,0:T(8,128)(2,1)}), bf16[32,128,576]{2,1,0:T(8,128)(2,1)}) %all-gather.3.cloned.1.call-update) | async-done | bytes 4718608 | tf_op jit(solution)/shard_map/all_gather | solution.py:217
  68.4 10.7 %select_reduce_fusion = (f32[8,4,128]{2,1,0:T(4,128)S(1)}, f32[8,4,128,1024]{3,2,1,0:T(8,128)S(1)}) fusion(pred[8,1024]{1,0:T(8,128)(4,1)S(1)} %broadcast_compare_fusion, bf16[8,4,128,576]{3,2,1,0:T(8,128)(2,1)} %bitcast.114, bf16[8,1024,576]{1,2,0:T(8,128)(2,1)} %param.14), kind=kOutput, calls=%fused_computation.1 | convolution fusion | flops 4844417024 | bytes 30957568 | tf_op jit(solution)/shard_map/rqhd,rtd->rqht/dot_general | solution.py:220
  79.1 5.7 %copy-done.3 = f32[8,4,128,1024]{3,2,1,0:T(8,128)} copy-done((f32[8,4,128,1024]{3,2,1,0:T(8,128)}, f32[8,4,128,1024]{3,2,1,0:T(8,128)S(1)}, u32[]{:S(2)}) %copy-start.3) | copy-done | bytes 16777240
  84.8 4.4 %fusion = f32[8,4,128]{2,1,0:T(4,128)S(1)} fusion(f32[8,4,128,1024]{3,2,1,0:T(8,128)S(1)} %get-tuple-element.12, f32[8,4,128]{2,1,0:T(4,128)S(1)} %get-tuple-element.11, pred[8,1024]{1,0:T(8,128)(4,1)S(1)} %broadcast_compare_fusion), kind=kLoop, calls=%fused_computation.2 | loop fusion | flops 16773120 | bytes 16818176 | tf_op jit(solution)/shard_map/reduce_sum | solution.py:225
  91.3 3.3 all-to-all-start.2
  96.2 4.0 %all-to-all-done.2 = f32[8,1,512]{2,1,0:T(1,128)S(1)} async-done(((f32[8,1,512]{2,1,0:T(1,128)}), f32[8,1,512]{2,1,0:T(1,128)S(1)}, u32[]{:S(2)}, u32[]{:S(2)}) %all-to-all-start.2) | async-done | bytes 16416 | tf_op jit(solution)/shard_map/all_to_all | solution.py:235
  100.2 3.3 all-to-all-start
  103.6 12.4 %fusion.14 = bf16[8,4,128,512]{3,2,1,0:T(8,128)(2,1)} fusion(bf16[8,1024,576]{1,2,0:T(8,128)(2,1)} %param.14, f32[8,4,128,1024]{3,2,1,0:T(8,128)} %copy-done.3, f32[8,4,128]{2,1,0:T(4,128)S(1)} %get-tuple-element.11, pred[8,1024]{1,0:T(8,128)(4,1)S(1)} %broadcast_compare_fusion), kind=kOutput, calls=%fused_computation.18 | convolution fusion | flops 4313841664 | bytes 29384704 | tf_op jit(solution)/shard_map/rqht,rtk->rqhk/dot_general | solution.py:226
  116.0 6.5 %copy.79 = bf16[1,32,128,512]{3,1,0,2:T(8,128)(2,1)} copy(bf16[1,32,128,512]{3,2,1,0:T(8,128)(2,1)} %bitcast.94) | data formatting | bytes 8388608 | tf_op jit(solution)/shard_map/broadcast_in_dim;reshape | solution.py:236
  122.6 5.0 %all-to-all-start.1 = ((bf16[1,32,128,512]{3,1,0,2:T(8,128)(2,1)}), bf16[1,32,128,512]{3,1,0,2:T(8,128)(2,1)}, u32[]{:S(2)}, u32[]{:S(2)}) async-start(bf16[1,32,128,512]{3,1,0,2:T(8,128)(2,1)} %copy.79), calls=%async_computation.1 | async-start | bytes 8388608 | tf_op jit(solution)/shard_map/all_to_all | solution.py:236
  127.7 123.3 %all-gather = s32[32,4,8]{2,1,0:T(4,128)S(1)} all-gather(s32[1,4,8]{2,1,0:T(4,128)S(1)} %bitcast.113), channel_id=1, replica_groups=mesh['group'=4,'ctx'=8] {'group','ctx'}, dimensions={0}, use_global_device_ids=true | all-gather | bytes 4224 | tf_op jit(solution)/shard_map/all_gather | solution.py:213
  251.1 1.1 select_reduce_fusion.1
  254.2 2.8 fusion.8
  257.6 0.8 fusion.20
  259.1 12.1 %convolution_convert_fusion = bf16[32,7168]{1,0:T(8,128)(2,1)S(1)} fusion(bf16[2048,7168]{1,0:T(8,128)(2,1)} %param.18, bf16[16,4,8,128]{3,2,1,0:T(8,128)(2,1)S(1)} %fusion.22), kind=kOutput, calls=%fused_computation.17 | convolution fusion | flops 939753472 | bytes 29949952 | tf_op jit(solution)/shard_map/dot_general | solution.py:281
  271.4 9.5 %shard_map.140 = f32[224,128]{1,0:T(8,128)S(1)} custom-call(bf16[2,1,4,224,128]{4,3,2,1,0:T(8,128)(2,1)S(1)} %bitcast.93), custom_call_target="tpu_custom_call" | custom-call | tf_op jit(solution)/shard_map/pallas_call | solution.py:171
  281.9 16.3 %shard_map.141 = bf16[2,4,4,224,128]{4,3,2,1,0:T(8,128)(2,1)S(1)} custom-call(bf16[224,128]{1,0:T(8,128)(2,1)S(1)} %reshape.162.x_ref), custom_call_target="tpu_custom_call" | custom-call | tf_op jit(solution)/shard_map/pallas_call | solution.py:98
  298.1 1.5 copy.88
  299.6 2.9 reshape.163
  302.6 7.9 %fusion.49 = f32[128,1024]{1,0:T(8,128)S(1)} fusion(bf16[128,7168]{1,0:T(8,128)(2,1)S(1)} %reshape.163, bf16[7168,1024]{1,0:T(8,128)(2,1)} %param.23), kind=kOutput, calls=%fused_computation.76 | convolution fusion | flops 1879048192 | bytes 17039360 | tf_op jit(solution)/shard_map/dot_general | solution.py:301
  311.1 15.4 %fusion.4 = bf16[128,7168]{1,0:T(8,128)(2,1)} fusion(bf16[1024,7168]{1,0:T(8,128)(2,1)} %param.25, f32[128]{0:T(128)S(1)} %multiply_divide_fusion, bf16[128,7168]{1,0:T(8,128)(2,1)} %copy-done.2, bf16[7168,1024]{1,0:T(8,128)(2,1)} %param.24, f32[128,1024]{1,0:T(8,128)S(1)} %fusion.49), kind=kOutput, calls=%fused_computation.7 | convolution fusion | flops 3760717824 | bytes 33554944 | tf_op jit(solution)/shard_map/dot_general | solution.py:304
  326.5 3.9 %reshape.164 = bf16[4,4,2,224,128]{4,3,2,1,0:T(8,128)(2,1)} reshape(bf16[128,7168]{1,0:T(8,128)(2,1)} %fusion.4) | data formatting | bytes 3670016 | tf_op jit(solution)/shard_map/reshape | solution.py:305
  330.5 1.6 copy.104
  332.1 22.7 %shard_map.142 = f32[224,128]{1,0:T(8,128)S(1)} custom-call(bf16[2,4,4,224,128]{4,3,2,1,0:T(8,128)(2,1)S(1)} %bitcast.92), custom_call_target="tpu_custom_call" | custom-call | tf_op jit(solution)/shard_map/pallas_call | solution.py:171
  (62 shorter events, 11.0 us)
Async XLA Ops:
  7.2 251.3 %copy-start = (bf16[16,512,128]{2,1,0:T(8,128)(2,1)S(1)}, bf16[16,512,128]{2,1,0:T(8,128)(2,1)}, u32[]{:S(2)}) copy-start(bf16[16,512,128]{2,1,0:T(8,128)(2,1)} %param.17) | copy-start | bytes 6291460
  7.2 61.2 %all-gather.3.cloned.1.call-start = ((), (), s32[]{:S(2)}) async-start(), calls=%async_computation.3 | async-start | bytes 5898240 | tf_op jit(solution)/shard_map/all_gather | solution.py:217
  79.1 5.7 %copy-start.3 = (f32[8,4,128,1024]{3,2,1,0:T(8,128)}, f32[8,4,128,1024]{3,2,1,0:T(8,128)S(1)}, u32[]{:S(2)}) copy-start(f32[8,4,128,1024]{3,2,1,0:T(8,128)S(1)} %get-tuple-element.12) | copy-start | bytes 50331652
  91.3 8.9 %all-to-all-start.2 = ((f32[8,1,512]{2,1,0:T(1,128)}), f32[8,1,512]{2,1,0:T(1,128)S(1)}, u32[]{:S(2)}, u32[]{:S(2)}) async-start(f32[8,1,512]{2,1,0:T(1,128)} %reshape.177), calls=%async_computation.2 | async-start | bytes 32768 | tf_op jit(solution)/shard_map/all_to_all | solution.py:235
  100.2 22.3 %all-to-all-start = ((f32[8,1,512]{2,1,0:T(1,128)}), f32[8,1,512]{2,1,0:T(1,128)S(1)}, u32[]{:S(2)}, u32[]{:S(2)}) async-start(f32[8,1,512]{2,1,0:T(1,128)} %reshape.175), calls=%async_computation | async-start | bytes 32768 | tf_op jit(solution)/shard_map/all_to_all | solution.py:234
  116.0 11.6 %copy-start.6 = (bf16[32,576]{1,0:T(8,128)(2,1)S(1)}, bf16[32,576]{1,0:T(8,128)(2,1)}, u32[]{:S(2)}) copy-start(bf16[32,576]{1,0:T(8,128)(2,1)} %param.15) | copy-start | bytes 110596
  116.0 11.6 %copy-start.9 = (s32[4,8]{1,0:T(4,128)S(1)}, s32[4,8]{1,0:T(4,128)}, u32[]{:S(2)}) copy-start(s32[4,8]{1,0:T(4,128)} %param.22) | copy-start | bytes 388
  116.0 135.1 %copy-start.4 = (bf16[32,16,576]{2,1,0:T(8,128)(2,1)S(1)}, bf16[32,16,576]{2,1,0:T(8,128)(2,1)}, u32[]{:S(2)}) copy-start(bf16[32,16,576]{2,1,0:T(8,128)(2,1)} %param.13) | copy-start | bytes 1769476
  122.6 131.6 %all-to-all-start.1 = ((bf16[1,32,128,512]{3,1,0,2:T(8,128)(2,1)}), bf16[1,32,128,512]{3,1,0,2:T(8,128)(2,1)}, u32[]{:S(2)}, u32[]{:S(2)}) async-start(bf16[1,32,128,512]{3,1,0,2:T(8,128)(2,1)} %copy.79), calls=%async_computation.1 | async-start | bytes 8388608 | tf_op jit(solution)/shard_map/all_to_all | solution.py:236
  259.0 21.9 %copy-start.7 = (bf16[4,7168]{1,0:T(4,128)(2,1)S(1)}, bf16[4,7168]{1,0:T(4,128)(2,1)}, u32[]{:S(2)}) copy-start(bf16[4,7168]{1,0:T(4,128)(2,1)} %param.19) | copy-start | bytes 172036
  259.0 22.7 %copy-start.8 = (f32[7168]{0:T(1024)S(1)}, f32[7168]{0:T(1024)}, u32[]{:S(2)}) copy-start(f32[7168]{0:T(1024)} %param.20) | copy-start | bytes 86020
  302.5 8.0 %copy-start.2 = (bf16[128,7168]{1,0:T(8,128)(2,1)}, bf16[128,7168]{1,0:T(8,128)(2,1)S(1)}, u32[]{:S(2)}) copy-start(bf16[128,7168]{1,0:T(8,128)(2,1)S(1)} %reshape.163) | copy-start | bytes 5505028
  302.5 8.0 %copy-start.5 = (bf16[7168,16]{0,1:T(8,128)(2,1)S(1)}, bf16[7168,16]{0,1:T(8,128)(2,1)}, u32[]{:S(2)}) copy-start(bf16[7168,16]{0,1:T(8,128)(2,1)} %param.21) | copy-start | bytes 688132
  311.1 44.4 %copy-start.1 = (bf16[16,512,128]{2,1,0:T(8,128)(2,1)S(1)}, bf16[16,512,128]{2,1,0:T(8,128)(2,1)}, u32[]{:S(2)}) copy-start(bf16[16,512,128]{2,1,0:T(8,128)(2,1)} %param.17) | copy-start | bytes 6291460
Sparse Core Ops, SparseCore 0:
  9.6 58.6 all-gather.2

commit v2 on v1

--- a/solution.py
+++ b/solution.py
@@ -183,6 +183,165 @@
         compiler_params=pltpu.CompilerParams(
             collective_id=collective_id, has_side_effects=True, vmem_limit_bytes=32 * 2**20),
     )(x)
+
+
+def attend_kernel(depth, scale, q_ref, cache_ref, live_ref, got_ref, got_stat_ref, heads, part, stat, core_part, core_stat,
+                  merged, merged_stat, q_line_send, q_line_recv, q_core_send, q_core_recv, core_send, core_recv,
+                  line_send, line_recv):
+    g = lax.axis_index("group")
+    c = lax.axis_index("ctx")
+    z, k = c // 2, c % 2
+    requests, rows, _ = q_ref.shape
+    spread = lax.broadcasted_iota(jnp.int32, (rows, LANES), 1)
+
+    def chip(t):
+        at, bit = z, 1
+        while bit <= t:
+            if t & bit:
+                at = at + bit - 2 * bit * ((z // bit) % 2)
+            bit *= 2
+        return at
+
+    partner = (g, z * 2 + 1 - k)
+    owners = [(g, chip(t) * 2 + k) for t in range(depth)]
+    enter([partner] + owners[1:])
+
+    def remote(src, dst, send, recv, device):
+        return pltpu.make_async_remote_copy(
+            src_ref=src, dst_ref=dst, send_sem=send, recv_sem=recv, device_id=device, device_id_type=MESH)
+
+    sent = []
+
+    def go(copy):
+        copy.start()
+        sent.append(copy)
+
+    def held(t):
+        return q_ref if t == 0 else heads.at[t, k]
+
+    def q_line(t):
+        bit = 1 << (t.bit_length() - 1)
+        return remote(held(t - bit), heads.at[t, k], q_line_send.at[t], q_line_recv.at[t], owners[bit])
+
+    def q_core(t, half):
+        return remote(held(t), heads.at[t, half], q_core_send.at[t], q_core_recv.at[t], partner)
+
+    def results(t, half):
+        return (
+            remote(part.at[t, half], core_part.at[t], core_send.at[t, 0], core_recv.at[t, 0], partner),
+            remote(stat.at[t, half], core_stat.at[t], core_send.at[t, 1], core_recv.at[t, 1], partner),
+        )
+
+    def returns(t):
+        return (
+            remote(merged.at[t], got_ref.at[t], line_send.at[t, 0], line_recv.at[t, 0], owners[t]),
+            remote(merged_stat.at[t], got_stat_ref.at[t], line_send.at[t, 1], line_recv.at[t, 1], owners[t]),
+        )
+
+    def forward(t):
+        go(q_core(t, k))
+        bit = 1 if t == 0 else 1 << t.bit_length()
+        while t + bit < depth:
+            go(q_line(t + bit))
+            bit *= 2
+
+    def one(t, r):
+        both = jnp.concatenate([heads[t, 0, r], heads[t, 1, r]], axis=0)
+        keys = cache_ref[r]
+        score = scale * lax.dot_general(both, keys, (((1,), (1,)), ((), ())), preferred_element_type=jnp.float32)
+        live = live_ref[r] > 0.0
+        top = jnp.max(jnp.where(live, score, neg_floor), axis=-1, keepdims=True)
+        prob = jnp.exp(jnp.where(live, score - top, neg_floor))
+        total = jnp.sum(prob, axis=-1, keepdims=True)
+        out = jnp.dot(prob.astype(jnp.bfloat16), keys[:, :LATENT_WIDTH], preferred_element_type=jnp.float32)
+        out = out.astype(part.dtype)
+        for half in range(2):
+            span = slice(half * rows, (half + 1) * rows)
+            part[t, half, r] = out[span]
+            stat[t, half] = jnp.where(
+                spread == r, top[span], jnp.where(spread == requests + r, total[span], stat[t, half]))
+
+    def compute(t):
+        stat[t] = jnp.zeros(stat.shape[1:], jnp.float32)
+        if requests % 2 == 0:
+            def pair(i, carry):
+                one(t, 2 * i)
+                one(t, 2 * i + 1)
+                return carry
+            lax.fori_loop(0, requests // 2, pair, 0)
+        else:
+            def single(i, carry):
+                one(t, i)
+                return carry
+            lax.fori_loop(0, requests, single, 0)
+        for copy in results(t, 1 - k):
+            go(copy)
+
+    def merge(t):
+        for copy in results(t, k):
+            copy.wait_recv()
+        mine, other = stat[t, k], core_stat[t]
+        new = jnp.zeros((rows, LANES), jnp.float32)
+        for r in range(requests):
+            top_a, top_b = mine[:, r : r + 1], other[:, r : r + 1]
+            sum_a, sum_b = mine[:, requests + r : requests + r + 1], other[:, requests + r : requests + r + 1]
+            top = jnp.maximum(top_a, top_b)
+            keep_a, keep_b = jnp.exp(top_a - top), jnp.exp(top_b - top)
+            block = keep_a * part[t, k, r].astype(jnp.float32) + keep_b * core_part[t, r].astype(jnp.float32)
+            block = block.astype(merged.dtype)
+            if t == 0:
+                got_ref[0, r] = block
+            else:
+                merged[t, r] = block
+            new = jnp.where(
+                spread == r, top, jnp.where(spread == requests + r, keep_a * sum_a + keep_b * sum_b, new))
+        if t == 0:
+            got_stat_ref[0] = new
+        else:
+            merged_stat[t] = new
+            for copy in returns(t):
+                go(copy)
+
+    forward(0)
+    heads[0, k] = q_ref[...]
+    for t in range(depth):
+        if t > 0:
+            q_line(t).wait_recv()
+            forward(t)
+            merge(t - 1)
+        q_core(t, 1 - k).wait_recv()
+        compute(t)
+    merge(depth - 1)
+    for t in range(1, depth):
+        for copy in returns(t):
+            copy.wait_recv()
+    for copy in sent:
+        copy.wait_send()
+
+
+def attend(q, cache, live, depth, scale, collective_id):
+    requests, rows, features = q.shape
+    sems = pltpu.SemaphoreType.DMA
+    blocks = (depth, requests, rows, LATENT_WIDTH)
+    stats = (depth, rows, LANES)
+    vmem = pl.BlockSpec(memory_space=pltpu.VMEM)
+    return pl.pallas_call(
+        functools.partial(attend_kernel, depth, scale),
+        out_shape=(jax.ShapeDtypeStruct(blocks, jnp.bfloat16), jax.ShapeDtypeStruct(stats, jnp.float32)),
+        in_specs=[vmem] * 3,
+        out_specs=(vmem, vmem),
+        scratch_shapes=[
+            pltpu.VMEM((depth, 2, requests, rows, features), jnp.bfloat16),
+            pltpu.VMEM((depth, 2, requests, rows, LATENT_WIDTH), jnp.bfloat16),
+            pltpu.VMEM((depth, 2, rows, LANES), jnp.float32),
+            pltpu.VMEM(blocks, jnp.bfloat16),
+            pltpu.VMEM(stats, jnp.float32),
+            pltpu.VMEM(blocks, jnp.bfloat16),
+            pltpu.VMEM(stats, jnp.float32),
+        ] + [sems((depth,))] * 4 + [sems((depth, 2))] * 4,
+        compiler_params=pltpu.CompilerParams(
+            collective_id=collective_id, has_side_effects=True, vmem_limit_bytes=48 * 2**20),
+    )(q, cache, live)
 
 
 def local(
@@ -210,30 +369,15 @@
     request_batch = lengths.shape[0]
     draft_tokens = grouped_rows // request_batch
     block_len = cache.shape[1]
-    all_routes = lax.all_gather(routes, ("group", "ctx"), axis=0, tiled=True)
     positions = ctx_index * block_len + jnp.arange(block_len, dtype=jnp.int32)
-    live_mask = (positions[None, :] < lengths[:, None])[:, None, None, :]
-    compressed_keys = cache[:, :, :LATENT_WIDTH]
-    all_heads = lax.all_gather(query, "ctx", axis=1, tiled=True)
-    current_width = all_heads.shape[1]
-    shaped = all_heads.reshape(request_batch, draft_tokens, current_width, features)
-    scores = score_scale * jnp.einsum(
-        "rqhd,rtd->rqht", shaped, cache, preferred_element_type=jnp.float32
-    )
-    block_max = jnp.max(jnp.where(live_mask, scores, neg_floor), axis=-1)
-    probability = jnp.exp(jnp.where(live_mask, scores - block_max[..., None], neg_floor))
-    block_sum = jnp.sum(probability, axis=-1)
-    block_result = jnp.einsum(
-        "rqht,rtk->rqhk",
-        probability.astype(jnp.bfloat16),
-        compressed_keys,
-        preferred_element_type=jnp.float32,
-    ).astype(jnp.bfloat16)
-    swap = functools.partial(lax.all_to_all, axis_name="ctx", split_axis=2, concat_axis=0, tiled=True)
+    live = (positions[None, :] < lengths[:, None]).astype(jnp.float32)[:, None, :]
+    folded = query.reshape(request_batch, draft_tokens * local_heads, features)
+    results, stats = attend(folded, cache, live, depth, score_scale, 3)
+    stats = stats.transpose(0, 2, 1)
     arrived = (
-        swap(block_max.reshape(grouped_rows, current_width)[None]),
-        swap(block_sum.reshape(grouped_rows, current_width)[None]),
-        swap(block_result.reshape(grouped_rows, current_width, LATENT_WIDTH)[None]),
+        stats[:, :request_batch].reshape(depth, grouped_rows, local_heads),
+        stats[:, request_batch : 2 * request_batch].reshape(depth, grouped_rows, local_heads),
+        results.reshape(depth, grouped_rows, local_heads, LATENT_WIDTH),
     )
     cache_max = jnp.max(arrived[0], axis=0)
     factors = jnp.exp(arrived[0] - cache_max[None])
@@ -286,12 +430,16 @@
     stream_wide = stream.astype(jnp.float32)
     mean_square = jnp.mean(stream_wide * stream_wide, axis=-1, keepdims=True)
     normed = (stream_wide * lax.rsqrt(mean_square + norm_eps) * norm_gain).astype(jnp.bfloat16)
-    rows = all_rows(normed.reshape(block, LANES), group_count, depth, 1)
+    expert_ids = jnp.arange(EXPERTS, dtype=jnp.int32)
+    chosen = jnp.sum((routes[:, :, None] == expert_ids).astype(jnp.bfloat16), axis=1).reshape(1, -1)
+    chosen = jnp.pad(chosen, ((0, 15), (0, LANES - row_count * EXPERTS)))
+    sent = jnp.concatenate([normed.reshape(block, LANES), chosen], axis=0)
+    gathered = all_rows(sent, group_count, depth, 1).transpose(1, 2, 0, 3, 4)
     device_count = group_count * ctx_count
-    rows = rows.transpose(1, 2, 0, 3, 4).reshape(device_count * row_count, model_width)
+    rows = gathered[..., :block, :].reshape(device_count * row_count, model_width)
     gate_values = jax.nn.sigmoid(jnp.dot(rows, w_router, preferred_element_type=jnp.float32))
-    expert_ids = jnp.arange(EXPERTS, dtype=jnp.int32)
-    chosen = jnp.sum((all_routes[:, :, None] == expert_ids).astype(jnp.float32), axis=1)
+    chosen = gathered[..., block, : row_count * EXPERTS].reshape(device_count * row_count, EXPERTS)
+    chosen = chosen.astype(jnp.float32)
     picked = chosen * gate_values
     expert = (group_index * ctx_count + ctx_index) // (device_count // EXPERTS)
     own = (expert_ids == expert).astype(jnp.float32)

time: 363 us -> 237 us (0.65)
  blocking collectives: 123 us -> 0 us
  Pallas kernels: 48.4 us -> 163 us
  waiting for transfers between devices: 64.4 us -> 0 us
  matrix products: 61.6 us -> 40 us
  between operations: 14.5 us -> 0.94 us
  starting transfers between devices: 11.8 us -> 0 us
  other arithmetic: 12.6 us -> 5 us
    all_gather x1 -> x0, blocking collectives: 123 us -> none  [local(): all_routes = lax.all_gather(routes, ('group', 'ctx'), axis=0, tiled=True)]
    pallas_call x0 -> x1, Pallas kernels: none -> 103 us  [attend(): pl.pallas_call(functools.partial(attend_kernel, depth, scale), out_shape=...]
    all_gather x1 -> x0, waiting for transfers between devices: 59.7 us -> none  [local(): all_heads = lax.all_gather(query, 'ctx', axis=1, tiled=True)]
    dot_general x2 -> x0, matrix products: 23.1 us -> none  [the longest x1 12.4 us: local(): jnp.einsum('rqht,rtk->rqhk', probability.astype(jnp.bfloat16), compressed...]
    all_to_all x3 -> x0, starting transfers between devices: 11.7 us -> none  [the longest x1 5.05 us: local(): swap(block_result.reshape(grouped_rows, current_width, LATENT_WIDTH)[None])]
    pallas_call x2, Pallas kernels: 32.2 us -> 42.5 us  [summed_rows(): pl.pallas_call(functools.partial(scatter_kernel, planes, depth), out_shap...]
    unnamed x26 -> x19, local copies, waits for them, and re-layouts: 8.04 us -> 15.6 us
    another operation x3 -> x0, local copies, waits for them, and re-layouts: 6.72 us -> none  [the longest x1 6.52 us: local(): block_result.reshape(grouped_rows, current_width, LATENT_WIDTH)[None]]
  transfers between devices with their start and end apart: 4 -> 0, of which waited for: 2 -> 0; matrix products, arithmetic and copies ran while one was open for 7% -> 0% of each run, Pallas kernels for 0% -> 0%
where the time goes in v2:
time: 237 us
  Pallas kernels  163 us (69%)
  matrix products  40 us (17%)
  local copies, waits for them, and re-layouts  27.7 us (12%)
  other arithmetic  5 us (2%)
    pallas_call x1, Pallas kernels, attend(): pl.pallas_call(functools.partial(attend_kernel, depth, scale), out_shape=...  103 us
    pallas_call x2, Pallas kernels, summed_rows(): pl.pallas_call(functools.partial(scatter_kernel, planes, depth), out_shap...  42.5 us
    pallas_call x1, Pallas kernels, all_rows(): pl.pallas_call(functools.partial(gather_kernel, planes, depth), out_shape...  17.5 us
    unnamed x19, local copies, waits for them, and re-layouts  15.6 us
    dot_general x1, matrix products, local(): jnp.dot(hidden, w_down, preferred_element_type=jnp.float32)  15.2 us
    dot_general x1, matrix products, local(): jnp.dot(per_head_values, w_out, preferred_element_type=jnp.float32)  12.3 us
    dot_general x1, matrix products, local(): gate_sum = jnp.dot(rows, w_gate, preferred_element_type=jnp.float32)  7.82 us
    reshape x2, local copies, waits for them, and re-layouts, local(): mixed.astype(jnp.bfloat16).reshape(group_count, depth, 2, block, LANES)  5.78 us

profile of v2, /device:TPU:0, one launch (start us, length us, event | category | flops | bytes accessed | tf_op | source)
XLA Modules:
  0.0 236.6 jit_solution(15917975346811600828)
XLA Ops:
  0.7 0.9 compare_convert_fusion.live_ref
  1.6 14.2 %copy.56.cache_ref = bf16[8,1024,576]{2,1,0:T(8,128)(2,1)} copy(bf16[8,1024,576]{1,2,0:T(8,128)(2,1)} %param.14) | data formatting | bytes 18874368 | tf_op args[1]
  15.8 102.9 %shard_map.140 = (bf16[4,8,64,512]{3,2,1,0:T(8,128)(2,1)S(1)}, f32[4,64,128]{2,1,0:T(8,128)S(1)}) custom-call(bf16[8,64,576]{2,1,0:T(8,128)(2,1)S(1)} %bitcast.56, bf16[8,1024,576]{2,1,0:T(8,128)(2,1)} %copy.56.cache_ref, f32[8,1,1024]{2,1,0:T(1,128)S(1)} %compare_convert_fusion.live_ref), custom_call_target="tpu_custom_call" | custom-call | tf_op jit(solution)/shard_map/pallas_call | solution.py:328
  118.7 1.3 copy-done.2
  120.2 1.1 select_reduce_fusion
  121.3 0.1 fusion.25
  121.7 2.2 multiply_reduce_fusion
  123.9 0.8 fusion.2
  124.7 0.7 fusion.4
  125.4 12.3 %convolution_convert_fusion = bf16[32,7168]{1,0:T(8,128)(2,1)S(1)} fusion(bf16[2048,7168]{1,0:T(8,128)(2,1)} %param.18, bf16[16,4,8,128]{3,2,1,0:T(8,128)(2,1)S(1)} %fusion.4), kind=kOutput, calls=%fused_computation.2 | convolution fusion | flops 939753472 | bytes 29949952 | tf_op jit(solution)/shard_map/dot_general | solution.py:425
  137.7 0.2 reshape.196
  138.0 20.4 %shard_map.141 = f32[224,128]{1,0:T(8,128)S(1)} custom-call(bf16[2,1,4,224,128]{4,3,2,1,0:T(8,128)(2,1)S(1)} %bitcast.53), custom_call_target="tpu_custom_call" | custom-call | tf_op jit(solution)/shard_map/pallas_call | solution.py:171
  158.4 0.8 fusion.20
  159.6 17.5 %shard_map.142 = bf16[2,4,4,240,128]{4,3,2,1,0:T(8,128)(2,1)S(1)} custom-call(bf16[240,128]{1,0:T(8,128)(2,1)S(1)} %fusion.24.x_ref), custom_call_target="tpu_custom_call" | custom-call | tf_op jit(solution)/shard_map/pallas_call | solution.py:98
  177.1 0.1 slice.24
  177.2 1.4 copy.65
  178.7 3.9 %reshape.200 = bf16[128,7168]{1,0:T(8,128)(2,1)} reshape(bf16[4,4,2,224,128]{4,3,2,1,0:T(8,128)(2,1)} %copy.65) | data formatting | bytes 3670016 | tf_op jit(solution)/shard_map/reshape | solution.py:439
  182.6 7.8 %fusion.34 = f32[128,1024]{1,0:T(8,128)S(1)} fusion(bf16[128,7168]{1,0:T(8,128)(2,1)} %reshape.200, bf16[7168,1024]{1,0:T(8,128)(2,1)} %param.23), kind=kOutput, calls=%fused_computation.66 | convolution fusion | flops 1879048192 | bytes 17039360 | tf_op jit(solution)/shard_map/dot_general | solution.py:449
  190.6 2.1 multiply_reduce_fusion.1
  192.8 15.2 %fusion = bf16[128,7168]{1,0:T(8,128)(2,1)} fusion(bf16[1024,7168]{1,0:T(8,128)(2,1)} %param.25, f32[128]{0:T(128)S(1)} %multiply_divide_fusion, bf16[128,7168]{1,0:T(8,128)(2,1)} %reshape.200, bf16[7168,1024]{1,0:T(8,128)(2,1)} %param.24, f32[128,1024]{1,0:T(8,128)S(1)} %fusion.34), kind=kOutput, calls=%fused_computation.1 | convolution fusion | flops 3760717824 | bytes 33554944 | tf_op jit(solution)/shard_map/dot_general | solution.py:452
  208.0 4.1 %reshape.201 = bf16[4,4,2,224,128]{4,3,2,1,0:T(8,128)(2,1)} reshape(bf16[128,7168]{1,0:T(8,128)(2,1)} %fusion) | data formatting | bytes 3670016 | tf_op jit(solution)/shard_map/reshape | solution.py:453
  212.1 1.6 copy.79
  213.8 22.1 %shard_map.143 = f32[224,128]{1,0:T(8,128)S(1)} custom-call(bf16[2,4,4,224,128]{4,3,2,1,0:T(8,128)(2,1)S(1)} %bitcast.52), custom_call_target="tpu_custom_call" | custom-call | tf_op jit(solution)/shard_map/pallas_call | solution.py:171
  236.0 0.7 fusion.23
  (43 shorter events, 1.1 us)
Async XLA Ops:
  0.6 124.1 %copy-start = (bf16[16,512,128]{2,1,0:T(8,128)(2,1)S(1)}, bf16[16,512,128]{2,1,0:T(8,128)(2,1)}, u32[]{:S(2)}) copy-start(bf16[16,512,128]{2,1,0:T(8,128)(2,1)} %param.17) | copy-start | bytes 6291460
  1.6 14.2 %copy-start.3 = (bf16[32,16,576]{2,1,0:T(8,128)(2,1)S(1)}, bf16[32,16,576]{2,1,0:T(8,128)(2,1)}, u32[]{:S(2)}) copy-start(bf16[32,16,576]{2,1,0:T(8,128)(2,1)} %param.13) | copy-start | bytes 1769476
  15.8 104.4 %copy-start.5 = (bf16[32,576]{1,0:T(8,128)(2,1)S(1)}, bf16[32,576]{1,0:T(8,128)(2,1)}, u32[]{:S(2)}) copy-start(bf16[32,576]{1,0:T(8,128)(2,1)} %param.15) | copy-start | bytes 110596
  118.7 1.4 copy-start.2
  125.4 33.0 %copy-start.6 = (bf16[4,7168]{1,0:T(4,128)(2,1)S(1)}, bf16[4,7168]{1,0:T(4,128)(2,1)}, u32[]{:S(2)}) copy-start(bf16[4,7168]{1,0:T(4,128)(2,1)} %param.19) | copy-start | bytes 172036
  125.4 33.8 %copy-start.7 = (f32[7168]{0:T(1024)S(1)}, f32[7168]{0:T(1024)}, u32[]{:S(2)}) copy-start(f32[7168]{0:T(1024)} %param.20) | copy-start | bytes 86020
  125.4 34.0 %copy-start.8 = (s32[4,8]{1,0:T(4,128)S(1)}, s32[4,8]{1,0:T(4,128)}, u32[]{:S(2)}) copy-start(s32[4,8]{1,0:T(4,128)} %param.22) | copy-start | bytes 388
  182.6 8.0 %copy-start.4 = (bf16[7168,16]{0,1:T(8,128)(2,1)S(1)}, bf16[7168,16]{0,1:T(8,128)(2,1)}, u32[]{:S(2)}) copy-start(bf16[7168,16]{0,1:T(8,128)(2,1)} %param.21) | copy-start | bytes 688132
  208.0 28.6 %copy-start.1 = (bf16[16,512,128]{2,1,0:T(8,128)(2,1)S(1)}, bf16[16,512,128]{2,1,0:T(8,128)(2,1)}, u32[]{:S(2)}) copy-start(bf16[16,512,128]{2,1,0:T(8,128)(2,1)} %param.17) | copy-start | bytes 6291460

commit v3 on v2

--- a/solution.py
+++ b/solution.py
@@ -185,13 +185,15 @@
     )(x)
 
 
-def attend_kernel(depth, scale, q_ref, cache_ref, live_ref, got_ref, got_stat_ref, heads, part, stat, core_part, core_stat,
-                  merged, merged_stat, q_line_send, q_line_recv, q_core_send, q_core_recv, core_send, core_recv,
+def attend_kernel(depth, scale, q_ref, cache_ref, live_ref, got_ref, got_stat_ref, heads, held_cache, part, stat, core_part,
+                  core_stat, merged, merged_stat, cache_sem, q_line_send, q_line_recv, q_core_send, q_core_recv, core_send, core_recv,
                   line_send, line_recv):
     g = lax.axis_index("group")
     c = lax.axis_index("ctx")
     z, k = c // 2, c % 2
     requests, rows, _ = q_ref.shape
+    middle = requests // 2
+    chunks = (range(middle), range(middle, requests))
     spread = lax.broadcasted_iota(jnp.int32, (rows, LANES), 1)
 
     def chip(t):
@@ -226,63 +228,62 @@
     def q_core(t, half):
         return remote(held(t), heads.at[t, half], q_core_send.at[t], q_core_recv.at[t], partner)
 
-    def results(t, half):
+    def results(t, h, half):
+        span = pl.ds(chunks[h][0], len(chunks[h]))
         return (
-            remote(part.at[t, half], core_part.at[t], core_send.at[t, 0], core_recv.at[t, 0], partner),
-            remote(stat.at[t, half], core_stat.at[t], core_send.at[t, 1], core_recv.at[t, 1], partner),
+            remote(part.at[t, half, span], core_part.at[t, span], core_send.at[t, h, 0], core_recv.at[t, h, 0], partner),
+            remote(stat.at[t, h, half], core_stat.at[t, h], core_send.at[t, h, 1], core_recv.at[t, h, 1], partner),
         )
 
-    def returns(t):
-        return (
-            remote(merged.at[t], got_ref.at[t], line_send.at[t, 0], line_recv.at[t, 0], owners[t]),
-            remote(merged_stat.at[t], got_stat_ref.at[t], line_send.at[t, 1], line_recv.at[t, 1], owners[t]),
-        )
-
-    def forward(t):
-        go(q_core(t, k))
-        bit = 1 if t == 0 else 1 << t.bit_length()
+    def returns(t, h):
+        span = pl.ds(chunks[h][0], len(chunks[h]))
+        block = remote(
+            merged.at[t, span], got_ref.at[t, span], line_send.at[t, h], line_recv.at[t, h], owners[t])
+        if h == 0:
+            return (block,)
+        return (block, remote(merged_stat.at[t], got_stat_ref.at[t], line_send.at[t, 2], line_recv.at[t, 2], owners[t]))
+
+    def relay(t, bit):
         while t + bit < depth:
             go(q_line(t + bit))
             bit *= 2
 
     def one(t, r):
         both = jnp.concatenate([heads[t, 0, r], heads[t, 1, r]], axis=0)
-        keys = cache_ref[r]
-        score = scale * lax.dot_general(both, keys, (((1,), (1,)), ((), ())), preferred_element_type=jnp.float32)
+        keys = held_cache[r]
+        score = scale * jnp.dot(both, keys, preferred_element_type=jnp.float32)
         live = live_ref[r] > 0.0
         top = jnp.max(jnp.where(live, score, neg_floor), axis=-1, keepdims=True)
         prob = jnp.exp(jnp.where(live, score - top, neg_floor))
         total = jnp.sum(prob, axis=-1, keepdims=True)
-        out = jnp.dot(prob.astype(jnp.bfloat16), keys[:, :LATENT_WIDTH], preferred_element_type=jnp.float32)
+        out = lax.dot_general(
+            prob.astype(jnp.bfloat16), keys[:LATENT_WIDTH], (((1,), (1,)), ((), ())),
+            preferred_element_type=jnp.float32)
         out = out.astype(part.dtype)
         for half in range(2):
-            span = slice(half * rows, (half + 1) * rows)
-            part[t, half, r] = out[span]
-            stat[t, half] = jnp.where(
-                spread == r, top[span], jnp.where(spread == requests + r, total[span], stat[t, half]))
-
-    def compute(t):
-        stat[t] = jnp.zeros(stat.shape[1:], jnp.float32)
-        if requests % 2 == 0:
-            def pair(i, carry):
-                one(t, 2 * i)
-                one(t, 2 * i + 1)
-                return carry
-            lax.fori_loop(0, requests // 2, pair, 0)
-        else:
-            def single(i, carry):
-                one(t, i)
-                return carry
-            lax.fori_loop(0, requests, single, 0)
-        for copy in results(t, 1 - k):
+            part[t, half, r] = out[half * rows : (half + 1) * rows]
+        return top, total
+
+    def compute(t, h, between):
+        stats = jnp.zeros((2 * rows, LANES), jnp.float32)
+        lanes = lax.broadcasted_iota(jnp.int32, (2 * rows, LANES), 1)
+        for i, r in enumerate(chunks[h]):
+            if i == len(chunks[h]) // 2:
+                between()
+            top, total = one(t, r)
+            stats = jnp.where(lanes == r, top, jnp.where(lanes == requests + r, total, stats))
+        for half in range(2):
+            stat[t, h, half] = stats[half * rows : (half + 1) * rows]
+        for copy in results(t, h, 1 - k):
             go(copy)
 
-    def merge(t):
-        for copy in results(t, k):
+    def merge(t, h):
+        for copy in results(t, h, k):
             copy.wait_recv()
-        mine, other = stat[t, k], core_stat[t]
-        new = jnp.zeros((rows, LANES), jnp.float32)
-        for r in range(requests):
+        mine, other = stat[t, h, k], core_stat[t, h]
+        stat_ref = got_stat_ref if t == 0 else merged_stat
+        new = jnp.zeros((rows, LANES), jnp.float32) if h == 0 else stat_ref[t]
+        for r in chunks[h]:
             top_a, top_b = mine[:, r : r + 1], other[:, r : r + 1]
             sum_a, sum_b = mine[:, requests + r : requests + r + 1], other[:, requests + r : requests + r + 1]
             top = jnp.maximum(top_a, top_b)
@@ -295,25 +296,30 @@
                 merged[t, r] = block
             new = jnp.where(
                 spread == r, top, jnp.where(spread == requests + r, keep_a * sum_a + keep_b * sum_b, new))
-        if t == 0:
-            got_stat_ref[0] = new
-        else:
-            merged_stat[t] = new
-            for copy in returns(t):
+        stat_ref[t] = new
+        if t > 0:
+            for copy in returns(t, h):
                 go(copy)
 
-    forward(0)
+    go(q_core(0, k))
+    if depth > 1:
+        go(q_line(1))
+    load = pltpu.make_async_copy(cache_ref, held_cache, cache_sem)
+    load.start()
     heads[0, k] = q_ref[...]
+    load.wait()
     for t in range(depth):
         if t > 0:
             q_line(t).wait_recv()
-            forward(t)
-            merge(t - 1)
+            go(q_core(t, k))
+            relay(t, 1 << t.bit_length())
+            merge(t - 1, 1)
         q_core(t, 1 - k).wait_recv()
-        compute(t)
-    merge(depth - 1)
+        compute(t, 0, functools.partial(relay, 0, 2) if t == 0 else lambda: None)
+        compute(t, 1, functools.partial(merge, t, 0))
+    merge(depth - 1, 1)
     for t in range(1, depth):
-        for copy in returns(t):
+        for copy in returns(t, 0) + returns(t, 1):
             copy.wait_recv()
     for copy in sent:
         copy.wait_send()
@@ -328,17 +334,19 @@
     return pl.pallas_call(
         functools.partial(attend_kernel, depth, scale),
         out_shape=(jax.ShapeDtypeStruct(blocks, jnp.bfloat16), jax.ShapeDtypeStruct(stats, jnp.float32)),
-        in_specs=[vmem] * 3,
+        in_specs=[vmem, pl.BlockSpec(memory_space=pl.ANY), vmem],
         out_specs=(vmem, vmem),
         scratch_shapes=[
             pltpu.VMEM((depth, 2, requests, rows, features), jnp.bfloat16),
+            pltpu.VMEM(cache.shape, jnp.bfloat16),
             pltpu.VMEM((depth, 2, requests, rows, LATENT_WIDTH), jnp.bfloat16),
+            pltpu.VMEM((depth, 2, 2, rows, LANES), jnp.float32),
+            pltpu.VMEM(blocks, jnp.bfloat16),
             pltpu.VMEM((depth, 2, rows, LANES), jnp.float32),
             pltpu.VMEM(blocks, jnp.bfloat16),
             pltpu.VMEM(stats, jnp.float32),
-            pltpu.VMEM(blocks, jnp.bfloat16),
-            pltpu.VMEM(stats, jnp.float32),
-        ] + [sems((depth,))] * 4 + [sems((depth, 2))] * 4,
+            sems,
+        ] + [sems((depth,))] * 4 + [sems((depth, 2, 2))] * 2 + [sems((depth, 3))] * 2,
         compiler_params=pltpu.CompilerParams(
             collective_id=collective_id, has_side_effects=True, vmem_limit_bytes=48 * 2**20),
     )(q, cache, live)
@@ -372,7 +380,7 @@
     positions = ctx_index * block_len + jnp.arange(block_len, dtype=jnp.int32)
     live = (positions[None, :] < lengths[:, None]).astype(jnp.float32)[:, None, :]
     folded = query.reshape(request_batch, draft_tokens * local_heads, features)
-    results, stats = attend(folded, cache, live, depth, score_scale, 3)
+    results, stats = attend(folded, cache.transpose(0, 2, 1), live, depth, score_scale, 3)
     stats = stats.transpose(0, 2, 1)
     arrived = (
         stats[:, :request_batch].reshape(depth, grouped_rows, local_heads),

time: 237 us -> 225 us (0.949)
  local copies, waits for them, and re-layouts: 27.7 us -> 15 us
    unnamed x19 -> x14, local copies, waits for them, and re-layouts: 15.6 us -> 2.46 us
where the time goes in v3:
time: 225 us
  Pallas kernels  165 us (73%)
  matrix products  38.4 us (17%)
  local copies, waits for them, and re-layouts  15 us (7%)
  other arithmetic  5.68 us (3%)
    pallas_call x1, Pallas kernels, attend(): pl.pallas_call(functools.partial(attend_kernel, depth, scale), out_shape=...  105 us
    pallas_call x2, Pallas kernels, summed_rows(): pl.pallas_call(functools.partial(scatter_kernel, planes, depth), out_shap...  42.2 us
    pallas_call x1, Pallas kernels, all_rows(): pl.pallas_call(functools.partial(gather_kernel, planes, depth), out_shape...  17.6 us
    dot_general x1, matrix products, local(): jnp.dot(hidden, w_down, preferred_element_type=jnp.float32)  14.7 us
    dot_general x1, matrix products, local(): jnp.dot(per_head_values, w_out, preferred_element_type=jnp.float32)  12.3 us
    dot_general x1, matrix products, local(): gate_sum = jnp.dot(rows, w_gate, preferred_element_type=jnp.float32)  7.24 us
    reshape x2, local copies, waits for them, and re-layouts, local(): mixed.astype(jnp.bfloat16).reshape(group_count, depth, 2, block, LANES)  5.73 us

profile of v3, /device:TPU:0, one launch (start us, length us, event | category | flops | bytes accessed | tf_op | source)
XLA Modules:
  0.0 224.9 jit_solution(12970852523003385975)
XLA Ops:
  0.7 0.9 fusion.31
  1.7 0.7 compare_convert_fusion.live_ref
  2.4 0.8 reshape.204
  3.2 0.8 reshape.192
  4.0 2.1 select_reduce_fusion
  6.2 1.1 copy-done.3
  7.3 105.1 %shard_map.140 = (bf16[4,8,64,512]{3,2,1,0:T(8,128)(2,1)S(1)}, f32[4,64,128]{2,1,0:T(8,128)S(1)}) custom-call(bf16[8,64,576]{2,1,0:T(8,128)(2,1)S(1)} %bitcast.58, bf16[8,576,1024]{2,1,0:T(8,128)(2,1)} %bitcast.59, f32[8,1,1024]{2,1,0:T(1,128)S(1)} %compare_convert_fusion.live_ref), custom_call_target="tpu_custom_call" | custom-call | tf_op jit(solution)/shard_map/pallas_call | solution.py:334
  112.4 1.3 copy-done.2
  114.3 2.2 multiply_reduce_fusion
  116.4 0.8 fusion.2
  117.3 0.6 fusion.4
  117.9 12.3 %convolution_convert_fusion = bf16[32,7168]{1,0:T(8,128)(2,1)S(1)} fusion(bf16[2048,7168]{1,0:T(8,128)(2,1)} %param.18, bf16[16,4,8,128]{3,2,1,0:T(8,128)(2,1)S(1)} %fusion.4), kind=kOutput, calls=%fused_computation.2 | convolution fusion | flops 939753472 | bytes 29949952 | tf_op jit(solution)/shard_map/dot_general | solution.py:433
  130.5 19.2 %shard_map.141 = f32[224,128]{1,0:T(8,128)S(1)} custom-call(bf16[2,1,4,224,128]{4,3,2,1,0:T(8,128)(2,1)S(1)} %bitcast.54), custom_call_target="tpu_custom_call" | custom-call | tf_op jit(solution)/shard_map/pallas_call | solution.py:171
  149.8 0.8 fusion.20
  150.7 17.6 %shard_map.142 = bf16[2,4,4,240,128]{4,3,2,1,0:T(8,128)(2,1)S(1)} custom-call(bf16[240,128]{1,0:T(8,128)(2,1)S(1)} %fusion.24.x_ref), custom_call_target="tpu_custom_call" | custom-call | tf_op jit(solution)/shard_map/pallas_call | solution.py:98
  168.5 1.5 copy.60
  169.9 2.8 %reshape.200 = bf16[128,7168]{1,0:T(8,128)(2,1)S(1)} reshape(bf16[4,4,2,224,128]{4,3,2,1,0:T(8,128)(2,1)} %copy.60) | data formatting | bytes 3670016 | tf_op jit(solution)/shard_map/reshape | solution.py:447
  172.9 0.6 multiply_reduce_fusion.1
  173.5 7.2 %fusion.34 = f32[128,1024]{1,0:T(8,128)S(1)} fusion(bf16[128,7168]{1,0:T(8,128)(2,1)S(1)} %reshape.200, bf16[7168,1024]{1,0:T(8,128)(2,1)} %param.23), kind=kOutput, calls=%fused_computation.66 | convolution fusion | flops 1879048192 | bytes 17039360 | tf_op jit(solution)/shard_map/dot_general | solution.py:457
  180.8 14.7 %fusion = bf16[128,7168]{1,0:T(8,128)(2,1)} fusion(bf16[1024,7168]{1,0:T(8,128)(2,1)} %param.25, f32[128]{0:T(128)S(1)} %multiply_divide_fusion, bf16[128,7168]{1,0:T(8,128)(2,1)S(1)} %reshape.200, bf16[7168,1024]{1,0:T(8,128)(2,1)} %param.24, f32[128,1024]{1,0:T(8,128)S(1)} %fusion.34), kind=kOutput, calls=%fused_computation.1 | convolution fusion | flops 3760717824 | bytes 33554944 | tf_op jit(solution)/shard_map/dot_general | solution.py:460
  195.5 3.9 %reshape.201 = bf16[4,4,2,224,128]{4,3,2,1,0:T(8,128)(2,1)} reshape(bf16[128,7168]{1,0:T(8,128)(2,1)} %fusion) | data formatting | bytes 3670016 | tf_op jit(solution)/shard_map/reshape | solution.py:461
  199.4 1.8 copy.74
  201.2 23.0 %shard_map.143 = f32[224,128]{1,0:T(8,128)S(1)} custom-call(bf16[2,4,4,224,128]{4,3,2,1,0:T(8,128)(2,1)S(1)} %bitcast.53), custom_call_target="tpu_custom_call" | custom-call | tf_op jit(solution)/shard_map/pallas_call | solution.py:171
  224.2 0.7 fusion.23
  (38 shorter events, 1.4 us)
Async XLA Ops:
  0.6 116.7 %copy-start = (bf16[16,512,128]{2,1,0:T(8,128)(2,1)S(1)}, bf16[16,512,128]{2,1,0:T(8,128)(2,1)}, u32[]{:S(2)}) copy-start(bf16[16,512,128]{2,1,0:T(8,128)(2,1)} %param.17) | copy-start | bytes 6291460
  6.2 1.1 copy-start.3
  112.4 1.4 copy-start.2
  130.2 19.5 %copy-start.5 = (bf16[4,7168]{1,0:T(4,128)(2,1)S(1)}, bf16[4,7168]{1,0:T(4,128)(2,1)}, u32[]{:S(2)}) copy-start(bf16[4,7168]{1,0:T(4,128)(2,1)} %param.19) | copy-start | bytes 172036
  130.2 20.3 %copy-start.6 = (f32[7168]{0:T(1024)S(1)}, f32[7168]{0:T(1024)}, u32[]{:S(2)}) copy-start(f32[7168]{0:T(1024)} %param.20) | copy-start | bytes 86020
  169.9 2.9 %copy-start.4 = (bf16[7168,16]{0,1:T(8,128)(2,1)S(1)}, bf16[7168,16]{0,1:T(8,128)(2,1)}, u32[]{:S(2)}) copy-start(bf16[7168,16]{0,1:T(8,128)(2,1)} %param.21) | copy-start | bytes 688132
  199.4 25.5 %copy-start.1 = (bf16[16,512,128]{2,1,0:T(8,128)(2,1)S(1)}, bf16[16,512,128]{2,1,0:T(8,128)(2,1)}, u32[]{:S(2)}) copy-start(bf16[16,512,128]{2,1,0:T(8,128)(2,1)} %param.17) | copy-start | bytes 6291460
